TPU v7x, 256 devices: a whole 4x4x8 slice. The times are simulated.
256 devices in a mesh: shot: 32 (over z, y_hi, core), surf: 8 (over y_lo, x).
Axes of the slice: x: 4, y: 4 (y_hi: 2, y_lo: 2; y = y_hi * 2 + y_lo), z: 8, core: 2. Of those that a mesh axis runs over, the one named last changes fastest.
Arguments:
- shot_data: float32 [2, 2, 6144, 2048], P(None, None, 'shot', 'surf'), may hold values from -6 to 6
- surface_data: float32 [2, 2, 2048, 4096], P(None, None, 'surf', 'shot'), may hold values from -0.1875 to 0.1875
Outputs:
- multiples: float32 [2, 2, 6144, 4096], P(None, None, 'shot', 'surf')
All inputs are finite; a program needn't handle non-finite values.
Results may differ from a plain program's by a relative error of at most 0.0001.
Values sent between devices are 32-bit elements; how exact they have to be, the bound alone decides.
No kernel may reach another device: no remote copies, remote signals or barrier semaphores. Data moves between devices by JAX's collectives and lax.ppermute only.
A program may use at most 128 MiB of HBM per device.

v0:
```python
import jax
import jax.numpy as jnp
from jax import lax
from jax.sharding import PartitionSpec as P


def stacked_left(shot_block):
    real_left = shot_block[0]
    imag_left = shot_block[1]
    upper = jnp.concatenate([real_left, -imag_left], axis=1)
    lower = jnp.concatenate([imag_left, real_left], axis=1)
    return jnp.concatenate([upper, lower], axis=0)


def columns_of(left, piece):
    right = piece.reshape(2 * piece.shape[1], piece.shape[2])
    return jnp.dot(left, right, precision=lax.Precision.HIGHEST, preferred_element_type=jnp.float32)


def on_device(shot_data, surface_data):
    freqs = shot_data.shape[0]
    rows = shot_data.shape[2]
    lefts = [stacked_left(shot_data[frequency]) for frequency in range(freqs)]
    results = []
    for frequency in range(freqs):

        def project(piece, start, left=lefts[frequency]):
            return columns_of(left, piece)

        partial_sum = project(
            lax.all_gather(surface_data[frequency], "shot", axis=2, tiled=True), jnp.int32(0)
        )
        partial_sum = partial_sum.reshape(2, rows, partial_sum.shape[1])
        results.append(lax.psum_scatter(partial_sum, "surf", scatter_dimension=2, tiled=True))
    return jnp.stack(results)


def solution(mesh):
    return jax.shard_map(
        on_device,
        mesh=mesh,
        in_specs=(P(None, None, "shot", "surf"), P(None, None, "surf", "shot")),
        out_specs=P(None, None, "shot", "surf"),
        check_vma=False,
    )
```

profile of v0, /device:TPU:1, one launch (start us, length us, event | category | flops | bytes accessed | tf_op | source)
XLA Modules:
  0.0 389.6 jit_solution(10190747548196959778)
XLA Ops:
  6.5 0.0 all-gather.5.cloned.1.call-start
  6.5 1.8 fusion.2
  8.4 0.0 all-gather.5.cloned.1.call-update
  8.4 0.0 all-gather.7.cloned.1.call-start
  8.5 0.7 all-gather.7.cloned.1.call-update
  9.2 0.0 reduce-scatter.3.cloned.1.call-start
  9.2 1.1 fusion
  10.3 1.3 slice_bitcast_fusion.2
  11.5 0.1 maximum_maximum_fusion
  11.6 110.9 %all-gather.5.cloned.1.call-done = f32[1,2,256,4096]{3,2,1,0:T(8,128)} async-done(((f32[1,2,256,128]{3,2,1,0:T(8,128)}), f32[1,2,256,4096]{3,2,1,0:T(8,128)}) %all-gather.5.cloned.1.call-update) | async-done | bytes 8388624 | tf_op jit(solution)/shard_map/all_gather | solution.py:31
  122.5 14.3 %fusion.3 = f32[2,192,4096]{2,1,0:T(8,128)} fusion(f32[2,192,512]{2,1,0:T(8,128)S(1)} %bitcast.28, f32[512,4096,1]{1,0,2:T(8,128)} %bitcast.27), kind=kOutput, calls=%fused_computation.10 | convolution fusion | flops 9663676416 | bytes 15466496 | tf_op jit(solution)/shard_map/dot_general | solution.py:17
  136.8 0.0 reduce-scatter.3.cloned.1.call-update
  136.8 0.0 reduce-scatter.5.cloned.1.call-start
  136.9 0.1 maximum_maximum_fusion.1
  137.0 92.9 %all-gather.7.cloned.1.call-done = f32[1,2,256,4096]{3,2,1,0:T(8,128)} async-done(((f32[1,2,256,128]{3,2,1,0:T(8,128)}), f32[1,2,256,4096]{3,2,1,0:T(8,128)}) %all-gather.7.cloned.1.call-update) | async-done | bytes 8388624 | tf_op jit(solution)/shard_map/all_gather | solution.py:31
  229.8 14.3 %fusion.4 = f32[2,192,4096]{2,1,0:T(8,128)} fusion(f32[2,192,512]{2,1,0:T(8,128)S(1)} %bitcast.29, f32[512,4096,1]{1,0,2:T(8,128)} %bitcast.26), kind=kOutput, calls=%fused_computation.11 | convolution fusion | flops 9663676416 | bytes 15466496 | tf_op jit(solution)/shard_map/dot_general | solution.py:17
  244.1 0.0 reduce-scatter.5.cloned.1.call-update
  244.1 59.7 %reduce-scatter.3.cloned.1.call-done = f32[2,192,512]{2,1,0:T(8,128)} async-done(((f32[2,192,4096]{2,1,0:T(8,128)}), f32[2,192,512]{2,1,0:T(8,128)}) %reduce-scatter.3.cloned.1.call-update) | async-done | bytes 786448 | tf_op jit(solution)/shard_map/reduce_scatter | solution.py:34
  303.8 76.7 %reduce-scatter.5.cloned.1.call-done = f32[2,192,512]{2,1,0:T(8,128)} async-done(((f32[2,192,4096]{2,1,0:T(8,128)}), f32[2,192,512]{2,1,0:T(8,128)}) %reduce-scatter.5.cloned.1.call-update) | async-done | bytes 786448 | tf_op jit(solution)/shard_map/reduce_scatter | solution.py:34
  380.5 2.6 pad_maximum_fusion
Async XLA Ops:
  6.5 116.0 %all-gather.5.cloned.1.call-start = ((), (), s32[]{:S(2)}) async-start(), calls=%async_computation.4 | async-start | bytes 8650752 | tf_op jit(solution)/shard_map/all_gather | solution.py:31
  8.4 221.4 %all-gather.7.cloned.1.call-start = ((), (), s32[]{:S(2)}) async-start(), calls=%async_computation.5 | async-start | bytes 8650752 | tf_op jit(solution)/shard_map/all_gather | solution.py:31
  9.2 294.6 %reduce-scatter.3.cloned.1.call-start = ((), (), s32[]{:S(2)}) async-start(), calls=%async_computation.2 | async-start | bytes 7077888 | tf_op jit(solution)/shard_map/reduce_scatter | solution.py:34
  136.8 243.6 %reduce-scatter.5.cloned.1.call-start = ((), (), s32[]{:S(2)}) async-start(), calls=%async_computation.3 | async-start | bytes 7077888 | tf_op jit(solution)/shard_map/reduce_scatter | solution.py:34
Sparse Core Ops, SparseCore 0:
  9.9 112.5 all-gather.4
  125.1 104.6 all-gather.6
  232.4 71.3 reduce-scatter.2
  306.2 74.2 reduce-scatter.4
where the time goes:
time: 390 us
  waiting for transfers between devices  341 us (87%)
  matrix products  28.5 us (7%)
  between operations  13.1 us (3%)
    all_gather x2, waiting for transfers between devices, on_device(): lax.all_gather(surface_data[frequency], 'shot', axis=2, tiled=True)  204 us
    reduce_scatter x2, waiting for transfers between devices, on_device(): lax.psum_scatter(partial_sum, 'surf', scatter_dimension=2, tiled=True)  136 us
    dot_general x2, matrix products, columns_of(): jnp.dot(left, right, precision=lax.Precision.HIGHEST, preferred_element_t...  28.5 us
  transfers between devices with their start and end apart: 4, of which 4 were waited for; matrix products, arithmetic and copies ran while one was open for 8% of the time, Pallas kernels for 0%

commit v1 on v0

v1 whole, which is shorter than its diff:
```python
import functools

import jax
import jax.numpy as jnp
from jax import lax
from jax.experimental import pallas as pl
from jax.experimental.pallas import tpu as pltpu
from jax.sharding import PartitionSpec as P

AXES = ("shot", "surf")
NX, NZ = 4, 8


def device_id(x, y_lo, y_hi, z, core):
    return ((z * 2 + y_hi) * 2 + core) * (2 * NX) + y_lo * NX + x


def coordinates():
    return [
        (x, y_lo, y_hi, z, core)
        for x in range(NX)
        for y_lo in range(2)
        for y_hi in range(2)
        for z in range(NZ)
        for core in range(2)
    ]


def move(array, where):
    pairs = [(device_id(*at), device_id(*where(*at))) for at in coordinates()]
    return lax.ppermute(array, AXES, pairs)


def along_z(array, step):
    return move(array, lambda x, yl, yh, z, c: (x, yl, yh, (z + step) % NZ, c))


def along_x(array, step):
    return move(array, lambda x, yl, yh, z, c: ((x + step) % NX, yl, yh, z, c))


def flip_y(array, lo, hi):
    return move(array, lambda x, yl, yh, z, c: (x, yl ^ lo, yh ^ hi, z, c))


def swap_cores(array):
    return move(array, lambda x, yl, yh, z, c: (x, yl, yh, z, c ^ 1))


def home_z(z, y_hi, core):
    return (z % NX - 1 + core + 2 * (z // NX) + 4 * y_hi) % NZ


def spread(piece, freq_of_x):
    return move(
        piece, lambda x, yl, yh, z, c: (z % NX, yl, freq_of_x(x), home_z(z, yh, c), x // 2)
    )


def split_kernel(place, *refs):
    *blocks, high_ref, low_ref = refs
    rows, depth = blocks[0].shape[1:]
    for half in range(2):
        for step in range(NX):
            for part in range(2):
                value = blocks[half * NX + step][part]
                high = value.astype(jnp.bfloat16)
                low = (value - high.astype(jnp.float32)).astype(jnp.bfloat16)
                at = pl.ds(pl.multiple_of(place[step] * (2 * depth) + part * depth, depth), depth)
                high_ref[half * rows : (half + 1) * rows, at] = high
                low_ref[half * rows : (half + 1) * rows, at] = low


def split_shots(place, blocks):
    rows, depth = blocks[0].shape[1:]
    out = jax.ShapeDtypeStruct((2 * rows, NX * 2 * depth), jnp.bfloat16)
    return pl.pallas_call(
        split_kernel,
        out_shape=(out, out),
        in_specs=[pl.BlockSpec(memory_space=pltpu.SMEM)]
        + [pl.BlockSpec(memory_space=pltpu.VMEM)] * len(blocks),
        out_specs=(pl.BlockSpec(memory_space=pltpu.VMEM),) * 2,
        compiler_params=pltpu.CompilerParams(vmem_limit_bytes=32 * 1024 * 1024),
        cost_estimate=pl.CostEstimate(flops=0, bytes_accessed=rows * depth * 128, transcendentals=0),
        name="split_shots",
    )(place, *blocks)


def product_kernel(flag, high_ref, low_ref, *refs):
    pieces = refs[:4]
    own, over_hi, over_lo, over_both, w_high, w_low = refs[4:]
    depth, columns = pieces[0].shape[2:]
    rows = own.shape[1]
    second = flag[0] == 1
    for side in range(2):
        for position in range(NX):
            core, slot = position // 2, position % 2
            first_group, second_group = pieces[core], pieces[2 + core]
            if side:
                first_group, second_group = second_group, first_group
            real = jnp.where(second, second_group[slot, 0], first_group[slot, 0])
            imag = jnp.where(second, second_group[slot, 1], first_group[slot, 1])
            real_high, imag_high = real.astype(jnp.bfloat16), imag.astype(jnp.bfloat16)
            real_low = (real - real_high.astype(jnp.float32)).astype(jnp.bfloat16)
            imag_low = (imag - imag_high.astype(jnp.float32)).astype(jnp.bfloat16)
            for to, r, i in ((w_high, real_high, imag_high), (w_low, real_low, imag_low)):
                base = position * 2 * depth
                to[side, base : base + depth, :columns] = r
                to[side, base : base + depth, columns:] = i
                to[side, base + depth : base + 2 * depth, :columns] = -i
                to[side, base + depth : base + 2 * depth, columns:] = r
        dot = functools.partial(jnp.dot, preferred_element_type=jnp.float32)
        total = (
            dot(high_ref[...], w_low[side]) + dot(low_ref[...], w_high[side])
        ) + dot(high_ref[...], w_high[side])
        near, far = (over_lo, over_both) if side else (own, over_hi)
        near[0], near[1] = total[:rows, :columns], total[:rows, columns:]
        far[0], far[1] = total[rows:, :columns], total[rows:, columns:]


def products(flag, high, low, pieces):
    rows = high.shape[0] // 2
    _, _, depth, columns = pieces[0].shape
    out = jax.ShapeDtypeStruct((2, rows, columns), jnp.float32)
    weights = pltpu.VMEM((2, NX * 2 * depth, 2 * columns), jnp.bfloat16)
    flops = 2 * 3 * high.shape[0] * high.shape[1] * 4 * columns
    return pl.pallas_call(
        product_kernel,
        out_shape=(out,) * 4,
        in_specs=[pl.BlockSpec(memory_space=pltpu.SMEM)]
        + [pl.BlockSpec(memory_space=pltpu.VMEM)] * 6,
        out_specs=(pl.BlockSpec(memory_space=pltpu.VMEM),) * 4,
        scratch_shapes=[weights, weights],
        compiler_params=pltpu.CompilerParams(vmem_limit_bytes=40 * 1024 * 1024),
        cost_estimate=pl.CostEstimate(flops=flops, bytes_accessed=7 << 20, transcendentals=0),
        name="products",
    )(flag, high, low, *pieces)


def finish_kernel(table, *refs):
    *parts, out_ref = refs
    columns = parts[0].shape[2]
    mine = table[0]
    for batch in range(len(parts) // 4):
        own, from_lo, from_hi, from_both = parts[4 * batch : 4 * batch + 4]
        at = pl.ds(pl.multiple_of(table[1 + batch] * columns, columns), columns)
        for part in range(2):
            out_ref[mine, part, :, at] = own[part] + from_lo[part]
            out_ref[1 - mine, part, :, at] = from_hi[part] + from_both[part]


def finish(table, parts):
    _, rows, columns = parts[0].shape
    shape = (2, 2, rows, columns * len(parts) // 4)
    return pl.pallas_call(
        finish_kernel,
        out_shape=jax.ShapeDtypeStruct(shape, jnp.float32),
        in_specs=[pl.BlockSpec(memory_space=pltpu.SMEM)]
        + [pl.BlockSpec(memory_space=pltpu.VMEM)] * len(parts),
        out_specs=pl.BlockSpec(memory_space=pltpu.VMEM),
        compiler_params=pltpu.CompilerParams(vmem_limit_bytes=32 * 1024 * 1024),
        cost_estimate=pl.CostEstimate(flops=0, bytes_accessed=5 << 20, transcendentals=0),
        name="finish",
    )(table, *parts)


def on_device(shot_data, surface_data):
    shot, surf = lax.axis_index("shot"), lax.axis_index("surf")
    z, y_hi, core = shot // 4, (shot // 2) % 2, shot % 2
    y_lo, x = surf // NX, surf % NX

    even = x % 2
    slot0 = spread(lax.dynamic_index_in_dim(surface_data, even, keepdims=False), lambda x: x % 2)
    slot1 = spread(lax.dynamic_index_in_dim(surface_data, 1 - even, keepdims=False), lambda x: 1 - x % 2)
    here = jnp.stack([slot0, slot1])

    mine = lax.dynamic_index_in_dim(shot_data, y_hi, keepdims=False)
    theirs = flip_y(lax.dynamic_index_in_dim(shot_data, 1 - y_hi, keepdims=False), 0, 1)
    blocks = [mine] + [along_x(mine, step) for step in range(1, NX)]
    blocks += [theirs] + [along_x(theirs, step) for step in range(1, NX)]
    sources = [(x - step) % NX for step in range(NX)]
    place = jnp.stack([2 * ((s // 2) ^ core) + ((s % 2) ^ y_hi) for s in sources]).astype(jnp.int32)
    high, low = split_shots(place, blocks)

    held = {0: here}
    up = down = here
    for step in range(1, NZ // 2):
        up, down = along_z(up, 1), along_z(down, -1)
        held[-step], held[step] = up, down
    held[NZ // 2] = jnp.stack([along_z(up[0], 1), along_z(down[1], -1)])
    both = {distance: (piece, swap_cores(piece)) for distance, piece in held.items()}

    parts, table = [], [y_hi]
    for one, two in ((-1, 1), (0, 2), (-3, 3), (-2, 4)):
        ranks = [(z + distance - x + 1) % NZ for distance in (one, two)]
        sides = [(rank // 2) % 2 for rank in ranks]
        flag = (sides[0] != y_lo).astype(jnp.int32)
        own, over_hi, over_lo, over_both = products(flag[None], high, low, both[one] + both[two])
        parts += [own, flip_y(over_lo, 1, 0), flip_y(over_hi, 0, 1), flip_y(over_both, 1, 1)]
        rank = jnp.where(flag == 1, ranks[1], ranks[0])
        table.append(rank % 2 + 2 * (rank // 4))
    return finish(jnp.stack(table).astype(jnp.int32), parts)


def solution(mesh):
    return jax.shard_map(
        on_device,
        mesh=mesh,
        in_specs=(P(None, None, "shot", "surf"), P(None, None, "surf", "shot")),
        out_specs=P(None, None, "shot", "surf"),
        check_vma=False,
    )
```

time: 390 us -> 161 us (0.41)
  waiting for transfers between devices: 341 us -> 44.4 us
  starting transfers between devices: 0.12 us -> 92.1 us
  matrix products: 28.5 us -> 0 us
  Pallas kernels: 0 us -> 18 us
  between operations: 13.1 us -> 0.25 us
    all_gather x2 -> x0, waiting for transfers between devices: 204 us -> none  [on_device(): lax.all_gather(surface_data[frequency], 'shot', axis=2, tiled=True)]
    reduce_scatter x2 -> x0, waiting for transfers between devices: 136 us -> none  [on_device(): lax.psum_scatter(partial_sum, 'surf', scatter_dimension=2, tiled=True)]
    ppermute x0 -> x37, starting transfers between devices: none -> 92.1 us  [move(): return lax.ppermute(array, AXES, pairs)]
    ppermute x0 -> x37, waiting for transfers between devices: none -> 44.4 us  [move(): return lax.ppermute(array, AXES, pairs)]
    dot_general x2 -> x0, matrix products: 28.5 us -> none  [columns_of(): jnp.dot(left, right, precision=lax.Precision.HIGHEST, preferred_element_t...]
    pallas_call x0 -> x6, Pallas kernels: none -> 18 us  [the longest x4 15 us: products(): pl.pallas_call(product_kernel, out_shape=(out,) * 4, in_specs=[pl.BlockSp...]
  transfers between devices with their start and end apart: 4 -> 37, of which waited for: 4 -> 14; matrix products, arithmetic and copies ran while one was open for 8% -> 1% of each run, Pallas kernels for 0% -> 10%
where the time goes in v1:
time: 161 us
  starting transfers between devices  92.1 us (57%)
  waiting for transfers between devices  44.4 us (28%)
  Pallas kernels  18 us (11%)
  local copies, waits for them, and re-layouts  4.61 us (3%)
    ppermute x37, starting transfers between devices, move(): return lax.ppermute(array, AXES, pairs)  92.1 us
    ppermute x37, waiting for transfers between devices, move(): return lax.ppermute(array, AXES, pairs)  44.4 us
    pallas_call x4, Pallas kernels, products(): pl.pallas_call(product_kernel, out_shape=(out,) * 4, in_specs=[pl.BlockSp...  15 us
  transfers between devices with their start and end apart: 37, of which 14 were waited for; matrix products, arithmetic and copies ran while one was open for 1% of the time, Pallas kernels for 10%

profile of v1, /device:TPU:1, one launch (start us, length us, event | category | flops | bytes accessed | tf_op | source)
XLA Modules:
  0.0 160.5 jit_solution(7808020308653122565)
XLA Ops:
  1.1 6.2 %collective-permute-start.8 = (f32[2,256,128]{2,1,0:T(8,128)S(1)}, f32[2,256,128]{2,1,0:T(8,128)S(1)}, u32[]{:S(2)}, u32[]{:S(2)}) collective-permute-start(f32[2,256,128]{2,1,0:T(8,128)S(1)} %get-tuple-element.44), channel_id=1, source_target_pairs={{0,240},{8,16},{32,17},{40,49},{64,50},{72,82},{96,83},{104,115},{... | collective-permute-start | bytes 786440 | tf_op jit(solution)/shard_map/ppermute | solution.py:31
  7.4 7.6 %collective-permute-start.7 = (f32[2,256,128]{2,1,0:T(8,128)S(1)}, f32[2,256,128]{2,1,0:T(8,128)S(1)}, u32[]{:S(2)}, u32[]{:S(2)}) collective-permute-start(f32[2,256,128]{2,1,0:T(8,128)S(1)} %get-tuple-element.43), channel_id=1, source_target_pairs={{0,224},{8,0},{32,1},{40,33},{64,34},{72,66},{96,67},{104,99},{128... | collective-permute-start | bytes 786440 | tf_op jit(solution)/shard_map/ppermute | solution.py:31
  16.1 12.9 %collective-permute-start.11 = (f32[2,2,256,128]{3,2,1,0:T(8,128)S(1)}, f32[2,2,256,128]{3,2,1,0:T(8,128)S(1)}, u32[]{:S(2)}, u32[]{:S(2)}) collective-permute-start(f32[2,2,256,128]{3,2,1,0:T(8,128)S(1)} %pad_maximum_fusion.refs_0_), channel_id=1, source_target_pairs={{0,224},{8,232},{32,0},{40,8},{64,32},{72,40},{96,64},{104,72},{12... | collective-permute-start | bytes 1572872 | tf_op jit(solution)/shard_map/ppermute | solution.py:31
  29.0 10.0 %collective-permute-start.9 = (f32[2,2,256,128]{3,2,1,0:T(8,128)S(1)}, f32[2,2,256,128]{3,2,1,0:T(8,128)S(1)}, u32[]{:S(2)}, u32[]{:S(2)}) collective-permute-start(f32[2,2,256,128]{3,2,1,0:T(8,128)S(1)} %pad_maximum_fusion.refs_0_), channel_id=1, source_target_pairs={{0,32},{8,40},{32,64},{40,72},{64,96},{72,104},{96,128},{104,136},... | collective-permute-start | bytes 1572872 | tf_op jit(solution)/shard_map/ppermute | solution.py:31
  39.0 11.3 %collective-permute-done.11.refs_2_ = f32[2,2,256,128]{3,2,1,0:T(8,128)S(1)} collective-permute-done((f32[2,2,256,128]{3,2,1,0:T(8,128)S(1)}, f32[2,2,256,128]{3,2,1,0:T(8,128)S(1)}, u32[]{:S(2)}, u32[]{:S(2)}) %collective-permute-start.11) | collective-permute-done | bytes 524320 | tf_op jit(solution)/shard_map/ppermute | solution.py:31
  53.1 4.6 %collective-permute-start = (f32[2,192,256]{2,1,0:T(8,128)S(1)}, f32[2,192,256]{2,1,0:T(8,128)S(1)}, u32[]{:S(2)}, u32[]{:S(2)}) collective-permute-start(f32[2,192,256]{2,1,0:T(8,128)S(1)} %get-tuple-element.42.refs_0_), channel_id=1, source_target_pairs={{0,1},{8,9},{32,33},{40,41},{64,65},{72,73},{96,97},{104,105},{128... | collective-permute-start | bytes 1179656 | tf_op jit(solution)/shard_map/ppermute | solution.py:31
  57.7 3.7 %collective-permute-start.1 = (f32[2,192,256]{2,1,0:T(8,128)S(1)}, f32[2,192,256]{2,1,0:T(8,128)S(1)}, u32[]{:S(2)}, u32[]{:S(2)}) collective-permute-start(f32[2,192,256]{2,1,0:T(8,128)S(1)} %get-tuple-element.42.refs_0_), channel_id=1, source_target_pairs={{0,2},{8,10},{32,34},{40,42},{64,66},{72,74},{96,98},{104,106},{12... | collective-permute-start | bytes 1179656 | tf_op jit(solution)/shard_map/ppermute | solution.py:31
  62.3 3.3 %collective-permute-start.25 = (f32[2,2,256,128]{3,2,1,0:T(8,128)}, f32[2,2,256,128]{3,2,1,0:T(8,128)S(1)}, u32[]{:S(2)}, u32[]{:S(2)}) collective-permute-start(f32[2,2,256,128]{3,2,1,0:T(8,128)} %collective-permute-done.17.refs_2_), channel_id=1, source_target_pairs={{0,224},{8,232},{32,0},{40,8},{64,32},{72,40},{96,64},{104,72},{12... | collective-permute-start | bytes 1572872 | tf_op jit(solution)/shard_map/ppermute | solution.py:31
  69.6 4.4 %collective-permute-done.1.refs_2_ = f32[2,192,256]{2,1,0:T(8,128)S(1)} collective-permute-done((f32[2,192,256]{2,1,0:T(8,128)S(1)}, f32[2,192,256]{2,1,0:T(8,128)S(1)}, u32[]{:S(2)}, u32[]{:S(2)}) %collective-permute-start.1) | collective-permute-done | bytes 393248 | tf_op jit(solution)/shard_map/ppermute | solution.py:31
  73.9 5.9 %collective-permute-start.16 = (f32[2,2,256,128]{3,2,1,0:T(8,128)S(1)}, f32[2,2,256,128]{3,2,1,0:T(8,128)S(1)}, u32[]{:S(2)}, u32[]{:S(2)}) collective-permute-start(f32[2,2,256,128]{3,2,1,0:T(8,128)S(1)} %pad_maximum_fusion.refs_0_), channel_id=1, source_target_pairs={{0,8},{8,0},{32,40},{40,32},{64,72},{72,64},{96,104},{104,96},{128... | collective-permute-start | bytes 1572872 | tf_op jit(solution)/shard_map/ppermute | solution.py:31
  80.6 6.5 %collective-permute-start.5 = (f32[2,192,256]{2,1,0:T(8,128)S(1)}, f32[2,192,256]{2,1,0:T(8,128)S(1)}, u32[]{:S(2)}, u32[]{:S(2)}) collective-permute-start(f32[2,192,256]{2,1,0:T(8,128)S(1)} %collective-permute-done.3.refs_4_), channel_id=1, source_target_pairs={{0,2},{8,10},{32,34},{40,42},{64,66},{72,74},{96,98},{104,106},{12... | collective-permute-start | bytes 1179656 | tf_op jit(solution)/shard_map/ppermute | solution.py:31
  88.8 3.6 %collective-permute-start.10 = (f32[2,2,256,128]{3,2,1,0:T(8,128)}, f32[2,2,256,128]{3,2,1,0:T(8,128)}, u32[]{:S(2)}, u32[]{:S(2)}) collective-permute-start(f32[2,2,256,128]{3,2,1,0:T(8,128)} %copy-done.8), channel_id=1, source_target_pairs={{0,8},{8,0},{32,40},{40,32},{64,72},{72,64},{96,104},{104,96},{128... | collective-permute-start | bytes 1572872 | tf_op jit(solution)/shard_map/ppermute | solution.py:31
  97.6 4.3 %collective-permute-done.6.refs_7_ = f32[2,192,256]{2,1,0:T(8,128)S(1)} collective-permute-done((f32[2,192,256]{2,1,0:T(8,128)S(1)}, f32[2,192,256]{2,1,0:T(8,128)S(1)}, u32[]{:S(2)}, u32[]{:S(2)}) %collective-permute-start.6) | collective-permute-done | bytes 393248 | tf_op jit(solution)/shard_map/ppermute | solution.py:31
  111.2 4.0 %products.4 = (f32[2,192,128]{2,1,0:T(8,128)S(1)}, f32[2,192,128]{2,1,0:T(8,128)S(1)}, f32[2,192,128]{2,1,0:T(8,128)S(1)}, f32[2,192,128]{2,1,0:T(8,128)S(1)}) custom-call(s32[1]{0:T(128)} %bitcast.5.flag, bf16[384,2048]{1,0:T(8,128)(2,1)S(1)} %get-tuple-element.23.high_ref, bf16[384,2048]{1,0:T(8,128)(2,1)S(1)} %get-tuple-element.24.low_ref, ...), custom_call_target="tpu_custom_call" | custom-call | flops 2415919104 | bytes 7340032 | tf_op jit(solution)/shard_map/products/pallas_call | solution.py:127
  116.1 4.0 %products.5 = (f32[2,192,128]{2,1,0:T(8,128)S(1)}, f32[2,192,128]{2,1,0:T(8,128)S(1)}, f32[2,192,128]{2,1,0:T(8,128)S(1)}, f32[2,192,128]{2,1,0:T(8,128)S(1)}) custom-call(s32[1]{0:T(128)} %bitcast.16.flag, bf16[384,2048]{1,0:T(8,128)(2,1)S(1)} %get-tuple-element.23.high_ref, bf16[384,2048]{1,0:T(8,128)(2,1)S(1)} %get-tuple-element.24.low_ref, ...), custom_call_target="tpu_custom_call" | custom-call | flops 2415919104 | bytes 7340032 | tf_op jit(solution)/shard_map/products/pallas_call | solution.py:127
  120.1 3.0 %collective-permute-start.14 = (f32[2,192,128]{2,1,0:T(8,128)S(1)}, f32[2,192,128]{2,1,0:T(8,128)S(1)}, u32[]{:S(2)}, u32[]{:S(2)}) collective-permute-start(f32[2,192,128]{2,1,0:T(8,128)S(1)} %get-tuple-element.27), channel_id=1, source_target_pairs={{0,16},{8,24},{32,48},{40,56},{64,80},{72,88},{96,112},{104,120},{... | collective-permute-start | bytes 589832 | tf_op jit(solution)/shard_map/ppermute | solution.py:31
  123.3 3.5 %products.6 = (f32[2,192,128]{2,1,0:T(8,128)S(1)}, f32[2,192,128]{2,1,0:T(8,128)}, f32[2,192,128]{2,1,0:T(8,128)S(1)}, f32[2,192,128]{2,1,0:T(8,128)S(1)}) custom-call(s32[1]{0:T(128)} %bitcast.17.flag, bf16[384,2048]{1,0:T(8,128)(2,1)S(1)} %get-tuple-element.23.high_ref, bf16[384,2048]{1,0:T(8,128)(2,1)S(1)} %get-tuple-element.24.low_ref, ...), custom_call_target="tpu_custom_call" | custom-call | flops 2415919104 | bytes 7340032 | tf_op jit(solution)/shard_map/products/pallas_call | solution.py:127
  131.0 3.6 %products.7 = (f32[2,192,128]{2,1,0:T(8,128)S(1)}, f32[2,192,128]{2,1,0:T(8,128)}, f32[2,192,128]{2,1,0:T(8,128)}, f32[2,192,128]{2,1,0:T(8,128)}) custom-call(s32[1]{0:T(128)} %bitcast.18.flag, bf16[384,2048]{1,0:T(8,128)(2,1)S(1)} %get-tuple-element.23.high_ref, bf16[384,2048]{1,0:T(8,128)(2,1)S(1)} %get-tuple-element.24.low_ref, ...), custom_call_target="tpu_custom_call" | custom-call | flops 2415919104 | bytes 7340032 | tf_op jit(solution)/shard_map/products/pallas_call | solution.py:127
  134.6 3.6 %collective-permute-start.28 = (f32[2,192,128]{2,1,0:T(8,128)}, f32[2,192,128]{2,1,0:T(8,128)S(1)}, u32[]{:S(2)}, u32[]{:S(2)}) collective-permute-start(f32[2,192,128]{2,1,0:T(8,128)} %get-tuple-element.35), channel_id=1, source_target_pairs={{0,16},{8,24},{32,48},{40,56},{64,80},{72,88},{96,112},{104,120},{... | collective-permute-start | bytes 589832 | tf_op jit(solution)/shard_map/ppermute | solution.py:31
  138.7 3.0 %collective-permute-done.21.refs_7_ = f32[2,192,128]{2,1,0:T(8,128)S(1)} collective-permute-done((f32[2,192,128]{2,1,0:T(8,128)S(1)}, f32[2,192,128]{2,1,0:T(8,128)S(1)}, u32[]{:S(2)}, u32[]{:S(2)}) %collective-permute-start.21) | collective-permute-done | bytes 196640 | tf_op jit(solution)/shard_map/ppermute | solution.py:31
  143.5 3.7 %collective-permute-done.28.refs_10_ = f32[2,192,128]{2,1,0:T(8,128)S(1)} collective-permute-done((f32[2,192,128]{2,1,0:T(8,128)}, f32[2,192,128]{2,1,0:T(8,128)S(1)}, u32[]{:S(2)}, u32[]{:S(2)}) %collective-permute-start.28) | collective-permute-done | bytes 196640 | tf_op jit(solution)/shard_map/ppermute | solution.py:31
  147.2 3.0 %collective-permute-done.29.refs_11_ = f32[2,192,128]{2,1,0:T(8,128)S(1)} collective-permute-done((f32[2,192,128]{2,1,0:T(8,128)S(1)}, f32[2,192,128]{2,1,0:T(8,128)S(1)}, u32[]{:S(2)}, u32[]{:S(2)}) %collective-permute-start.29) | collective-permute-done | bytes 196640 | tf_op jit(solution)/shard_map/ppermute | solution.py:31
  150.2 5.4 %collective-permute-done.35.refs_14_ = f32[2,192,128]{2,1,0:T(8,128)S(1)} collective-permute-done((f32[2,192,128]{2,1,0:T(8,128)}, f32[2,192,128]{2,1,0:T(8,128)S(1)}, u32[]{:S(2)}, u32[]{:S(2)}) %collective-permute-start.35) | collective-permute-done | bytes 196640 | tf_op jit(solution)/shard_map/ppermute | solution.py:31
  155.6 3.0 %collective-permute-done.36.refs_15_ = f32[2,192,128]{2,1,0:T(8,128)S(1)} collective-permute-done((f32[2,192,128]{2,1,0:T(8,128)}, f32[2,192,128]{2,1,0:T(8,128)S(1)}, u32[]{:S(2)}, u32[]{:S(2)}) %collective-permute-start.36) | collective-permute-done | bytes 196640 | tf_op jit(solution)/shard_map/ppermute | solution.py:31
  (94 shorter events, 36.3 us)
Async XLA Ops:
  1.1 13.8 %collective-permute-start.8 = (f32[2,256,128]{2,1,0:T(8,128)S(1)}, f32[2,256,128]{2,1,0:T(8,128)S(1)}, u32[]{:S(2)}, u32[]{:S(2)}) collective-permute-start(f32[2,256,128]{2,1,0:T(8,128)S(1)} %get-tuple-element.44), channel_id=1, source_target_pairs={{0,240},{8,16},{32,17},{40,49},{64,50},{72,82},{96,83},{104,115},{... | collective-permute-start | bytes 786440 | tf_op jit(solution)/shard_map/ppermute | solution.py:31
  16.1 34.2 %collective-permute-start.11 = (f32[2,2,256,128]{3,2,1,0:T(8,128)S(1)}, f32[2,2,256,128]{3,2,1,0:T(8,128)S(1)}, u32[]{:S(2)}, u32[]{:S(2)}) collective-permute-start(f32[2,2,256,128]{3,2,1,0:T(8,128)S(1)} %pad_maximum_fusion.refs_0_), channel_id=1, source_target_pairs={{0,224},{8,232},{32,0},{40,8},{64,32},{72,40},{96,64},{104,72},{12... | collective-permute-start | bytes 1572872 | tf_op jit(solution)/shard_map/ppermute | solution.py:31
  29.0 24.0 %collective-permute-start.9 = (f32[2,2,256,128]{3,2,1,0:T(8,128)S(1)}, f32[2,2,256,128]{3,2,1,0:T(8,128)S(1)}, u32[]{:S(2)}, u32[]{:S(2)}) collective-permute-start(f32[2,2,256,128]{3,2,1,0:T(8,128)S(1)} %pad_maximum_fusion.refs_0_), channel_id=1, source_target_pairs={{0,32},{8,40},{32,64},{40,72},{64,96},{72,104},{96,128},{104,136},... | collective-permute-start | bytes 1572872 | tf_op jit(solution)/shard_map/ppermute | solution.py:31
  53.0 26.8 %collective-permute-start.22 = (f32[2,2,256,128]{3,2,1,0:T(8,128)S(1)}, f32[2,2,256,128]{3,2,1,0:T(8,128)S(1)}, u32[]{:S(2)}, u32[]{:S(2)}) collective-permute-start(f32[2,2,256,128]{3,2,1,0:T(8,128)S(1)} %collective-permute-done.9.refs_0_), channel_id=1, source_target_pairs={{0,32},{8,40},{32,64},{40,72},{64,96},{72,104},{96,128},{104,136},... | collective-permute-start | bytes 1572872 | tf_op jit(solution)/shard_map/ppermute | solution.py:31
  53.1 13.7 %collective-permute-start = (f32[2,192,256]{2,1,0:T(8,128)S(1)}, f32[2,192,256]{2,1,0:T(8,128)S(1)}, u32[]{:S(2)}, u32[]{:S(2)}) collective-permute-start(f32[2,192,256]{2,1,0:T(8,128)S(1)} %get-tuple-element.42.refs_0_), channel_id=1, source_target_pairs={{0,1},{8,9},{32,33},{40,41},{64,65},{72,73},{96,97},{104,105},{128... | collective-permute-start | bytes 1179656 | tf_op jit(solution)/shard_map/ppermute | solution.py:31
  57.7 16.3 %collective-permute-start.1 = (f32[2,192,256]{2,1,0:T(8,128)S(1)}, f32[2,192,256]{2,1,0:T(8,128)S(1)}, u32[]{:S(2)}, u32[]{:S(2)}) collective-permute-start(f32[2,192,256]{2,1,0:T(8,128)S(1)} %get-tuple-element.42.refs_0_), channel_id=1, source_target_pairs={{0,2},{8,10},{32,34},{40,42},{64,66},{72,74},{96,98},{104,106},{12... | collective-permute-start | bytes 1179656 | tf_op jit(solution)/shard_map/ppermute | solution.py:31
  62.3 24.8 %collective-permute-start.25 = (f32[2,2,256,128]{3,2,1,0:T(8,128)}, f32[2,2,256,128]{3,2,1,0:T(8,128)S(1)}, u32[]{:S(2)}, u32[]{:S(2)}) collective-permute-start(f32[2,2,256,128]{3,2,1,0:T(8,128)} %collective-permute-done.17.refs_2_), channel_id=1, source_target_pairs={{0,224},{8,232},{32,0},{40,8},{64,32},{72,40},{96,64},{104,72},{12... | collective-permute-start | bytes 1572872 | tf_op jit(solution)/shard_map/ppermute | solution.py:31
  65.7 14.2 %collective-permute-start.3 = (f32[2,192,256]{2,1,0:T(8,128)S(1)}, f32[2,192,256]{2,1,0:T(8,128)S(1)}, u32[]{:S(2)}, u32[]{:S(2)}) collective-permute-start(f32[2,192,256]{2,1,0:T(8,128)S(1)} %get-tuple-element.41), channel_id=1, source_target_pairs={{0,16},{8,24},{32,48},{40,56},{64,80},{72,88},{96,112},{104,120},{... | collective-permute-start | bytes 1179656 | tf_op jit(solution)/shard_map/ppermute | solution.py:31
  66.8 13.8 %collective-permute-start.2 = (f32[2,192,256]{2,1,0:T(8,128)S(1)}, f32[2,192,256]{2,1,0:T(8,128)S(1)}, u32[]{:S(2)}, u32[]{:S(2)}) collective-permute-start(f32[2,192,256]{2,1,0:T(8,128)S(1)} %get-tuple-element.42.refs_0_), channel_id=1, source_target_pairs={{0,3},{8,11},{32,35},{40,43},{64,67},{72,75},{96,99},{104,107},{12... | collective-permute-start | bytes 1179656 | tf_op jit(solution)/shard_map/ppermute | solution.py:31
  73.9 14.1 %collective-permute-start.16 = (f32[2,2,256,128]{3,2,1,0:T(8,128)S(1)}, f32[2,2,256,128]{3,2,1,0:T(8,128)S(1)}, u32[]{:S(2)}, u32[]{:S(2)}) collective-permute-start(f32[2,2,256,128]{3,2,1,0:T(8,128)S(1)} %pad_maximum_fusion.refs_0_), channel_id=1, source_target_pairs={{0,8},{8,0},{32,40},{40,32},{64,72},{72,64},{96,104},{104,96},{128... | collective-permute-start | bytes 1572872 | tf_op jit(solution)/shard_map/ppermute | solution.py:31
  79.9 14.7 %collective-permute-start.23 = (f32[2,2,256,128]{3,2,1,0:T(8,128)S(1)}, f32[2,2,256,128]{3,2,1,0:T(8,128)S(1)}, u32[]{:S(2)}, u32[]{:S(2)}) collective-permute-start(f32[2,2,256,128]{3,2,1,0:T(8,128)S(1)} %collective-permute-done.22.refs_0_), channel_id=1, source_target_pairs={{0,32},{8,40},{32,64},{40,72},{64,96},{72,104},{96,128},{104,136},... | collective-permute-start | bytes 1572872 | tf_op jit(solution)/shard_map/ppermute | solution.py:31
  79.9 16.3 %collective-permute-start.4 = (f32[2,192,256]{2,1,0:T(8,128)S(1)}, f32[2,192,256]{2,1,0:T(8,128)S(1)}, u32[]{:S(2)}, u32[]{:S(2)}) collective-permute-start(f32[2,192,256]{2,1,0:T(8,128)S(1)} %collective-permute-done.3.refs_4_), channel_id=1, source_target_pairs={{0,1},{8,9},{32,33},{40,41},{64,65},{72,73},{96,97},{104,105},{128... | collective-permute-start | bytes 1179656 | tf_op jit(solution)/shard_map/ppermute | solution.py:31
  80.6 17.0 %collective-permute-start.5 = (f32[2,192,256]{2,1,0:T(8,128)S(1)}, f32[2,192,256]{2,1,0:T(8,128)S(1)}, u32[]{:S(2)}, u32[]{:S(2)}) collective-permute-start(f32[2,192,256]{2,1,0:T(8,128)S(1)} %collective-permute-done.3.refs_4_), channel_id=1, source_target_pairs={{0,2},{8,10},{32,34},{40,42},{64,66},{72,74},{96,98},{104,106},{12... | collective-permute-start | bytes 1179656 | tf_op jit(solution)/shard_map/ppermute | solution.py:31
  87.1 14.8 %collective-permute-start.6 = (f32[2,192,256]{2,1,0:T(8,128)S(1)}, f32[2,192,256]{2,1,0:T(8,128)S(1)}, u32[]{:S(2)}, u32[]{:S(2)}) collective-permute-start(f32[2,192,256]{2,1,0:T(8,128)S(1)} %collective-permute-done.3.refs_4_), channel_id=1, source_target_pairs={{0,3},{8,11},{32,35},{40,43},{64,67},{72,75},{96,99},{104,107},{12... | collective-permute-start | bytes 1179656 | tf_op jit(solution)/shard_map/ppermute | solution.py:31
  88.8 21.8 %collective-permute-start.10 = (f32[2,2,256,128]{3,2,1,0:T(8,128)}, f32[2,2,256,128]{3,2,1,0:T(8,128)}, u32[]{:S(2)}, u32[]{:S(2)}) collective-permute-start(f32[2,2,256,128]{3,2,1,0:T(8,128)} %copy-done.8), channel_id=1, source_target_pairs={{0,8},{8,0},{32,40},{40,32},{64,72},{72,64},{96,104},{104,96},{128... | collective-permute-start | bytes 1572872 | tf_op jit(solution)/shard_map/ppermute | solution.py:31
  94.6 16.2 %collective-permute-start.12 = (f32[2,2,256,128]{3,2,1,0:T(8,128)}, f32[2,2,256,128]{3,2,1,0:T(8,128)}, u32[]{:S(2)}, u32[]{:S(2)}) collective-permute-start(f32[2,2,256,128]{3,2,1,0:T(8,128)} %copy-done.6), channel_id=1, source_target_pairs={{0,8},{8,0},{32,40},{40,32},{64,72},{72,64},{96,104},{104,96},{128... | collective-permute-start | bytes 1572872 | tf_op jit(solution)/shard_map/ppermute | solution.py:31
  102.7 12.6 %collective-permute-start.18 = (f32[2,2,256,128]{3,2,1,0:T(8,128)}, f32[2,2,256,128]{3,2,1,0:T(8,128)}, u32[]{:S(2)}, u32[]{:S(2)}) collective-permute-start(f32[2,2,256,128]{3,2,1,0:T(8,128)} %collective-permute-done.17.refs_2_), channel_id=1, source_target_pairs={{0,8},{8,0},{32,40},{40,32},{64,72},{72,64},{96,104},{104,96},{128... | collective-permute-start | bytes 1572872 | tf_op jit(solution)/shard_map/ppermute | solution.py:31
  107.2 12.9 %collective-permute-start.24 = (f32[2,2,256,128]{3,2,1,0:T(8,128)S(1)}, f32[2,2,256,128]{3,2,1,0:T(8,128)S(1)}, u32[]{:S(2)}, u32[]{:S(2)}) collective-permute-start(f32[2,2,256,128]{3,2,1,0:T(8,128)S(1)} %copy-done.5), channel_id=1, source_target_pairs={{0,8},{8,0},{32,40},{40,32},{64,72},{72,64},{96,104},{104,96},{128... | collective-permute-start | bytes 1572872 | tf_op jit(solution)/shard_map/ppermute | solution.py:31
  107.4 15.7 %collective-permute-start.26 = (f32[2,2,256,128]{3,2,1,0:T(8,128)S(1)}, f32[2,2,256,128]{3,2,1,0:T(8,128)S(1)}, u32[]{:S(2)}, u32[]{:S(2)}) collective-permute-start(f32[2,2,256,128]{3,2,1,0:T(8,128)S(1)} %copy-done.3), channel_id=1, source_target_pairs={{0,8},{8,0},{32,40},{40,32},{64,72},{72,64},{96,104},{104,96},{128... | collective-permute-start | bytes 1572872 | tf_op jit(solution)/shard_map/ppermute | solution.py:31
  110.6 20.1 %collective-permute-start.30 = (f32[2,2,256,128]{3,2,1,0:T(8,128)S(1)}, f32[2,2,256,128]{3,2,1,0:T(8,128)S(1)}, u32[]{:S(2)}, u32[]{:S(2)}) collective-permute-start(f32[2,2,256,128]{3,2,1,0:T(8,128)S(1)} %copy-done.11), channel_id=1, source_target_pairs={{0,8},{8,0},{32,40},{40,32},{64,72},{72,64},{96,104},{104,96},{128... | collective-permute-start | bytes 1572872 | tf_op jit(solution)/shard_map/ppermute | solution.py:31
  110.7 20.3 %collective-permute-start.33 = (f32[2,2,256,128]{3,2,1,0:T(8,128)S(1)}, f32[2,2,256,128]{3,2,1,0:T(8,128)S(1)}, u32[]{:S(2)}, u32[]{:S(2)}) collective-permute-start(f32[2,2,256,128]{3,2,1,0:T(8,128)S(1)} %pad_maximum_fusion.1.refs_2_), channel_id=1, source_target_pairs={{0,8},{8,0},{32,40},{40,32},{64,72},{72,64},{96,104},{104,96},{128... | collective-permute-start | bytes 1572872 | tf_op jit(solution)/shard_map/ppermute | solution.py:31
  134.6 12.6 %collective-permute-start.28 = (f32[2,192,128]{2,1,0:T(8,128)}, f32[2,192,128]{2,1,0:T(8,128)S(1)}, u32[]{:S(2)}, u32[]{:S(2)}) collective-permute-start(f32[2,192,128]{2,1,0:T(8,128)} %get-tuple-element.35), channel_id=1, source_target_pairs={{0,16},{8,24},{32,48},{40,56},{64,80},{72,88},{96,112},{104,120},{... | collective-permute-start | bytes 589832 | tf_op jit(solution)/shard_map/ppermute | solution.py:31
  141.7 13.9 %collective-permute-start.35 = (f32[2,192,128]{2,1,0:T(8,128)}, f32[2,192,128]{2,1,0:T(8,128)S(1)}, u32[]{:S(2)}, u32[]{:S(2)}) collective-permute-start(f32[2,192,128]{2,1,0:T(8,128)} %get-tuple-element.39), channel_id=1, source_target_pairs={{0,16},{8,24},{32,48},{40,56},{64,80},{72,88},{96,112},{104,120},{... | collective-permute-start | bytes 589832 | tf_op jit(solution)/shard_map/ppermute | solution.py:31
  142.1 16.5 %collective-permute-start.36 = (f32[2,192,128]{2,1,0:T(8,128)}, f32[2,192,128]{2,1,0:T(8,128)S(1)}, u32[]{:S(2)}, u32[]{:S(2)}) collective-permute-start(f32[2,192,128]{2,1,0:T(8,128)} %get-tuple-element.40), channel_id=1, source_target_pairs={{0,20},{8,28},{32,52},{40,60},{64,84},{72,92},{96,116},{104,124},{... | collective-permute-start | bytes 589832 | tf_op jit(solution)/shard_map/ppermute | solution.py:31
  (28 other events, 303.9 us)

commit v2 on v0

v2 whole, which is shorter than its diff:
```python
import functools

import jax
import jax.numpy as jnp
from jax import lax
from jax.experimental import pallas as pl
from jax.experimental.pallas import tpu as pltpu
from jax.sharding import PartitionSpec as P

AXES = ("shot", "surf")
NX, NZ = 4, 8
POINT_BLOCKS = 2 * NX


def device_id(x, y_lo, y_hi, z, core):
    return ((z * 2 + y_hi) * 2 + core) * (2 * NX) + y_lo * NX + x


def move(array, where):
    pairs = [
        (device_id(x, yl, yh, z, c), device_id(*where(x, yl, yh, z, c)))
        for x in range(NX)
        for yl in range(2)
        for yh in range(2)
        for z in range(NZ)
        for c in range(2)
    ]
    return lax.ppermute(array, AXES, pairs)


def along_x(array, step):
    return move(array, lambda x, yl, yh, z, c: ((x + step) % NX, yl, yh, z, c))


def flip_y(array, lo, hi):
    return move(array, lambda x, yl, yh, z, c: (x, yl ^ lo, yh ^ hi, z, c))


def spread(piece, number):
    freq, half = number // 2, number % 2
    return move(piece, lambda x, yl, yh, z, c: (yh + 2 * c, half ^ yl, freq ^ (x % 2), z, x // 2))


def gather_z(array):
    groups = [
        [device_id(x, yl, yh, z, c) for z in range(NZ) for c in range(2)]
        for yh in range(2)
        for yl in range(2)
        for x in range(NX)
    ]
    return lax.all_gather(array, AXES, axis_index_groups=groups, axis=0, tiled=True)


def exchange(array):
    groups = [
        [device_id(x, yl, yh, z, c) for yh in range(2) for yl in range(2) for x in range(NX)]
        for z in range(NZ)
        for c in range(2)
    ]
    return lax.all_to_all(array, AXES, 0, 0, axis_index_groups=groups, tiled=True)


def together(*arrays):
    return lax.optimization_barrier(arrays)


VMEM = pl.BlockSpec(memory_space=pltpu.VMEM)
ANY = pl.BlockSpec(memory_space=pl.ANY)


def place():
    surf, shot = lax.axis_index("surf"), lax.axis_index("shot")
    return lax.rem(surf, NX), lax.div(surf, NX), lax.rem(lax.div(shot, 2), 2)


def turned(value):
    return pltpu.roll(value, value.shape[1] // 2, 1)


def left(shape):
    return lax.broadcasted_iota(jnp.int32, shape, 1) < shape[1] // 2


def parts_of(value):
    high = value.astype(jnp.bfloat16)
    return high, (value - high.astype(jnp.float32)).astype(jnp.bfloat16)


def pack_kernel(surface, *pieces):
    x, y_lo, _ = place()
    for number in range(2):
        freq = number ^ lax.rem(x, 2)
        real, imag = surface[freq, 0], surface[freq, 1]
        first = jnp.where(left(real.shape), real, turned(imag))
        second = jnp.where(left(real.shape), turned(real), imag)
        pieces[2 * number][...] = jnp.where(y_lo == 0, first, second)
        pieces[2 * number + 1][...] = jnp.where(y_lo == 0, second, first)


def pack(surface_data):
    out = jax.ShapeDtypeStruct(surface_data.shape[2:], jnp.float32)
    return pl.pallas_call(
        pack_kernel,
        out_shape=(out,) * 4,
        in_specs=[VMEM],
        out_specs=(VMEM,) * 4,
        cost_estimate=pl.CostEstimate(flops=0, bytes_accessed=1 << 20, transcendentals=0),
        name="pack",
    )(surface_data)


def split_kernel(*refs):
    *blocks, high_ref, low_ref, held, arrived = refs
    _, _, _, rows, depth = held.shape
    copies = [
        pltpu.make_async_copy(block, held.at[number], arrived.at[number])
        for number, block in enumerate(blocks)
    ]
    for copy in copies:
        copy.start()
    for number, copy in enumerate(copies):
        copy.wait()
        for half in range(2):
            for part in range(2):
                first = (2 * part + half) * rows
                at = slice(first, first + rows), slice(number * depth, (number + 1) * depth)
                high_ref[at], low_ref[at] = parts_of(held[number, half, part])


def split_shots(blocks):
    _, _, rows, depth = blocks[0].shape
    out = jax.ShapeDtypeStruct((4 * rows, POINT_BLOCKS * depth), jnp.bfloat16)
    return pl.pallas_call(
        split_kernel,
        out_shape=(out, out),
        in_specs=[ANY] * len(blocks),
        out_specs=(VMEM,) * 2,
        scratch_shapes=[
            pltpu.VMEM((len(blocks), *blocks[0].shape), jnp.float32),
            pltpu.SemaphoreType.DMA((len(blocks),)),
        ],
        compiler_params=pltpu.CompilerParams(vmem_limit_bytes=12 * 1024 * 1024),
        cost_estimate=pl.CostEstimate(flops=0, bytes_accessed=12 << 20, transcendentals=0),
        name="split_shots",
    )(*blocks)


def product_kernel(gathered, high_ref, low_ref, out, w_high, w_low):
    rows = out.shape[1]
    points, columns = gathered.shape[1:]
    x, y_lo, y_hi = place()
    dot = functools.partial(jnp.dot, preferred_element_type=jnp.float32)
    for pair in range(NZ // 2):
        for side in range(2):
            for number in range(POINT_BLOCKS):
                across, step = number // NX, number % NX
                source = lax.rem(x + (NX - step), NX)
                freq = lax.rem(source, 2) ^ y_hi
                piece = (2 * pair + side) * 8 + lax.div(source, 2) * 4 + freq * 2 + across
                at = (
                    pair,
                    slice(number * points, (number + 1) * points),
                    slice(side * columns, (side + 1) * columns),
                )
                w_high[at], w_low[at] = parts_of(gathered[piece])
        total = (
            dot(high_ref[...], w_low[pair]) + dot(low_ref[...], w_high[pair])
        ) + dot(high_ref[...], w_high[pair])
        for side in range(2):
            at = slice(side * columns, (side + 1) * columns)
            real, imag = total[: 2 * rows, at], turned(total[2 * rows :, at])
            value = real + jnp.where(left(imag.shape), -imag, imag)
            out[y_hi * NZ + 2 * pair + side] = value[:rows]
            out[(1 - y_hi) * NZ + 2 * pair + side] = value[rows:]


def products(gathered, high, low):
    rows, depth = high.shape[0] // 4, high.shape[1]
    _, points, columns = gathered.shape
    flops = 2 * 3 * 4 * rows * depth * columns * NZ
    weights = pltpu.VMEM((NZ // 2, depth, 2 * columns), jnp.bfloat16)
    return pl.pallas_call(
        product_kernel,
        out_shape=jax.ShapeDtypeStruct((2 * NZ, rows, columns), jnp.float32),
        in_specs=[VMEM, VMEM, VMEM],
        out_specs=VMEM,
        scratch_shapes=[weights, weights],
        compiler_params=pltpu.CompilerParams(vmem_limit_bytes=30 * 1024 * 1024),
        cost_estimate=pl.CostEstimate(flops=flops, bytes_accessed=15 << 20, transcendentals=0),
        name="products",
    )(gathered, high, low)


def finish_kernel(came, out):
    columns = came.shape[2]
    for freq in range(2):
        for x in range(NX):
            first, second = came[freq * NZ + x], came[freq * NZ + NX + x]
            shard = 2 * (x % 2) + x // 2
            to = slice(shard * columns, (shard + 1) * columns)
            out[freq, 0, :, to] = jnp.where(left(first.shape), first, turned(second))
            out[freq, 1, :, to] = jnp.where(left(first.shape), turned(first), second)


def finish(came):
    _, rows, columns = came.shape
    return pl.pallas_call(
        finish_kernel,
        out_shape=jax.ShapeDtypeStruct((2, 2, rows, columns * NX), jnp.float32),
        in_specs=[VMEM],
        out_specs=VMEM,
        compiler_params=pltpu.CompilerParams(vmem_limit_bytes=16 * 1024 * 1024),
        cost_estimate=pl.CostEstimate(flops=0, bytes_accessed=3 << 20, transcendentals=0),
        name="finish",
    )(came)


def on_device(shot_data, surface_data):
    y_hi = (lax.axis_index("shot") // 2) % 2
    pieces = [spread(piece, number) for number, piece in enumerate(pack(surface_data))]
    mine = lax.dynamic_index_in_dim(shot_data, y_hi, keepdims=False)
    theirs = lax.dynamic_index_in_dim(shot_data, 1 - y_hi, keepdims=False)
    here, theirs = together(jnp.stack(pieces), flip_y(theirs, 0, 1))
    gathered = gather_z(here)

    block = jnp.stack([mine, theirs])
    across, up, down = together(flip_y(block, 1, 0), along_x(block, 1), along_x(block, -1))
    across_up, across_down, up = together(along_x(across, 1), along_x(across, -1), up)
    far, across_far = along_x(up, 1), along_x(across_down, -1)
    high, low = split_shots([block, up, far, down, across, across_up, across_far, across_down])
    return finish(exchange(products(gathered, high, low)))


def solution(mesh):
    return jax.shard_map(
        on_device,
        mesh=mesh,
        in_specs=(P(None, None, "shot", "surf"), P(None, None, "surf", "shot")),
        out_specs=P(None, None, "shot", "surf"),
        check_vma=False,
    )
```

time: 390 us -> 152 us (0.39)
  waiting for transfers between devices: 341 us -> 62.5 us
  matrix products: 28.5 us -> 0 us
  blocking collectives: 0 us -> 26.9 us
  starting transfers between devices: 0.12 us -> 21.8 us
  Pallas kernels: 0 us -> 16.1 us
  local copies, waits for them, and re-layouts: 3.12 us -> 8.14 us
    all_gather x2 -> x1, waiting for transfers between devices: 204 us -> 0.01 us  [gather_z(): lax.all_gather(array, AXES, axis_index_groups=groups, axis=0, tiled=True)]
    reduce_scatter x2 -> x0, waiting for transfers between devices: 136 us -> none  [on_device(): lax.psum_scatter(partial_sum, 'surf', scatter_dimension=2, tiled=True)]
    ppermute x0 -> x12, waiting for transfers between devices: none -> 62.5 us  [move(): return lax.ppermute(array, AXES, pairs)]
    dot_general x2 -> x0, matrix products: 28.5 us -> none  [columns_of(): jnp.dot(left, right, precision=lax.Precision.HIGHEST, preferred_element_t...]
    all_to_all x0 -> x1, blocking collectives: none -> 26.9 us  [exchange(): lax.all_to_all(array, AXES, 0, 0, axis_index_groups=groups, tiled=True)]
    ppermute x0 -> x12, starting transfers between devices: none -> 21.8 us  [move(): return lax.ppermute(array, AXES, pairs)]
    pallas_call x0 -> x4, Pallas kernels: none -> 16.1 us  [the longest x1 11 us: products(): pl.pallas_call(product_kernel, out_shape=jax.ShapeDtypeStruct((2 * NZ, ro...]
    unnamed x0 -> x6, local copies, waits for them, and re-layouts: none -> 6.97 us
  transfers between devices with their start and end apart: 4 -> 13, of which waited for: 4 -> 7; matrix products, arithmetic and copies ran while one was open for 8% -> 1% of each run, Pallas kernels for 0% -> 2%
where the time goes in v2:
time: 152 us; the launch traced here: 150 us
  waiting for transfers between devices  62.5 us (41%)
  blocking collectives  26.9 us (18%)
  starting transfers between devices  21.8 us (14%)
  Pallas kernels  16.1 us (11%)
  between operations  13.4 us (9%)
  local copies, waits for them, and re-layouts  8.14 us (5%)
    ppermute x12, waiting for transfers between devices, move(): return lax.ppermute(array, AXES, pairs)  62.5 us
    all_to_all x1, blocking collectives, exchange(): lax.all_to_all(array, AXES, 0, 0, axis_index_groups=groups, tiled=True)  26.9 us
    ppermute x12, starting transfers between devices, move(): return lax.ppermute(array, AXES, pairs)  21.8 us
    pallas_call x1, Pallas kernels, products(): pl.pallas_call(product_kernel, out_shape=jax.ShapeDtypeStruct((2 * NZ, ro...  11 us
    unnamed x6, local copies, waits for them, and re-layouts  6.97 us
  transfers between devices with their start and end apart: 13, of which 7 were waited for; matrix products, arithmetic and copies ran while one was open for 1% of the time, Pallas kernels for 2%

profile of v2, /device:TPU:1, one launch (start us, length us, event | category | flops | bytes accessed | tf_op | source)
XLA Modules:
  0.0 149.8 jit_solution(11407751131751239683)
XLA Ops:
  6.5 1.2 constant_dynamic-slice_fusion
  7.7 3.8 %collective-permute-start.4 = (f32[2,192,256]{2,1,0:T(8,128)S(1)}, f32[2,192,256]{2,1,0:T(8,128)S(1)}, u32[]{:S(2)}, u32[]{:S(2)}) collective-permute-start(f32[2,192,256]{2,1,0:T(8,128)S(1)} %get-tuple-element.34), channel_id=1, source_target_pairs={{0,16},{8,24},{32,48},{40,56},{64,80},{72,88},{96,112},{104,120},{... | collective-permute-start | bytes 1179656 | tf_op jit(solution)/shard_map/ppermute | solution.py:28
  11.5 2.0 %pack.1 = (f32[256,128]{1,0:T(8,128)}, f32[256,128]{1,0:T(8,128)}, f32[256,128]{1,0:T(8,128)}, f32[256,128]{1,0:T(8,128)}) custom-call(f32[2,2,256,128]{3,2,1,0:T(8,128)} %surface.1), custom_call_target="tpu_custom_call" | custom-call | bytes 1048576 | tf_op jit(solution)/shard_map/pack/pallas_call | solution.py:102
  13.5 5.5 %collective-permute-start = (f32[256,128]{1,0:T(8,128)}, f32[256,128]{1,0:T(8,128)S(1)}, u32[]{:S(2)}, u32[]{:S(2)}) collective-permute-start(f32[256,128]{1,0:T(8,128)} %get-tuple-element.19), channel_id=1, source_target_pairs={{0,0},{8,2},{32,32},{40,34},{64,64},{72,66},{96,96},{104,98},{128,... | collective-permute-start | bytes 393224 | tf_op jit(solution)/shard_map/ppermute | solution.py:28
  19.2 3.9 %collective-permute-start.2 = (f32[256,128]{1,0:T(8,128)}, f32[256,128]{1,0:T(8,128)S(1)}, u32[]{:S(2)}, u32[]{:S(2)}) collective-permute-start(f32[256,128]{1,0:T(8,128)} %get-tuple-element.21), channel_id=1, source_target_pairs={{0,16},{8,18},{32,48},{40,50},{64,80},{72,82},{96,112},{104,114},{... | collective-permute-start | bytes 393224 | tf_op jit(solution)/shard_map/ppermute | solution.py:28
  23.1 3.1 %collective-permute-done.1 = f32[256,128]{1,0:T(8,128)S(1)} collective-permute-done((f32[256,128]{1,0:T(8,128)}, f32[256,128]{1,0:T(8,128)S(1)}, u32[]{:S(2)}, u32[]{:S(2)}) %collective-permute-start.1) | collective-permute-done | bytes 131104 | tf_op jit(solution)/shard_map/ppermute | solution.py:28
  26.2 4.8 %collective-permute-done.2 = f32[256,128]{1,0:T(8,128)S(1)} collective-permute-done((f32[256,128]{1,0:T(8,128)}, f32[256,128]{1,0:T(8,128)S(1)}, u32[]{:S(2)}, u32[]{:S(2)}) %collective-permute-start.2) | collective-permute-done | bytes 131104 | tf_op jit(solution)/shard_map/ppermute | solution.py:28
  31.1 2.4 %collective-permute-done.3 = f32[256,128]{1,0:T(8,128)S(1)} collective-permute-done((f32[256,128]{1,0:T(8,128)}, f32[256,128]{1,0:T(8,128)S(1)}, u32[]{:S(2)}, u32[]{:S(2)}) %collective-permute-start.3) | collective-permute-done | bytes 131104 | tf_op jit(solution)/shard_map/ppermute | solution.py:28
  33.5 0.8 pad_maximum_fusion.1
  34.4 0.4 collective-permute-start.5
  34.7 2.7 %collective-permute-start.7 = (f32[2,2,192,256]{3,2,1,0:T(8,128)S(1)}, f32[2,2,192,256]{3,2,1,0:T(8,128)S(1)}, u32[]{:S(2)}, u32[]{:S(2)}) collective-permute-start(f32[2,2,192,256]{3,2,1,0:T(8,128)S(1)} %pad_maximum_fusion.refs_0_), channel_id=1, source_target_pairs={{0,3},{8,11},{32,35},{40,43},{64,67},{72,75},{96,99},{104,107},{12... | collective-permute-start | bytes 2359304 | tf_op jit(solution)/shard_map/ppermute | solution.py:28
  37.4 16.4 %collective-permute-done.5.refs_4_ = f32[2,2,192,256]{3,2,1,0:T(8,128)S(1)} collective-permute-done((f32[2,2,192,256]{3,2,1,0:T(8,128)S(1)}, f32[2,2,192,256]{3,2,1,0:T(8,128)S(1)}, u32[]{:S(2)}, u32[]{:S(2)}) %collective-permute-start.5) | collective-permute-done | bytes 786464 | tf_op jit(solution)/shard_map/ppermute | solution.py:28
  53.9 1.7 %collective-permute-done.6.refs_1_ = f32[2,2,192,256]{3,2,1,0:T(8,128)S(1)} collective-permute-done((f32[2,2,192,256]{3,2,1,0:T(8,128)S(1)}, f32[2,2,192,256]{3,2,1,0:T(8,128)S(1)}, u32[]{:S(2)}, u32[]{:S(2)}) %collective-permute-start.6) | collective-permute-done | bytes 786464 | tf_op jit(solution)/shard_map/ppermute | solution.py:28
  55.6 2.7 %collective-permute-start.9 = (f32[2,2,192,256]{3,2,1,0:T(8,128)S(1)}, f32[2,2,192,256]{3,2,1,0:T(8,128)S(1)}, u32[]{:S(2)}, u32[]{:S(2)}) collective-permute-start(f32[2,2,192,256]{3,2,1,0:T(8,128)S(1)} %collective-permute-done.5.refs_4_), channel_id=1, source_target_pairs={{0,3},{8,11},{32,35},{40,43},{64,67},{72,75},{96,99},{104,107},{12... | collective-permute-start | bytes 2359304 | tf_op jit(solution)/shard_map/ppermute | solution.py:28
  58.3 17.4 %collective-permute-done.8.refs_5_ = f32[2,2,192,256]{3,2,1,0:T(8,128)S(1)} collective-permute-done((f32[2,2,192,256]{3,2,1,0:T(8,128)S(1)}, f32[2,2,192,256]{3,2,1,0:T(8,128)S(1)}, u32[]{:S(2)}, u32[]{:S(2)}) %collective-permute-start.8) | collective-permute-done | bytes 786464 | tf_op jit(solution)/shard_map/ppermute | solution.py:28
  75.8 2.6 %collective-permute-start.11 = (f32[2,2,192,256]{3,2,1,0:T(8,128)S(1)}, f32[2,2,192,256]{3,2,1,0:T(8,128)S(1)}, u32[]{:S(2)}, u32[]{:S(2)}) collective-permute-start(f32[2,2,192,256]{3,2,1,0:T(8,128)S(1)} %collective-permute-done.9.refs_7_), channel_id=1, source_target_pairs={{0,3},{8,11},{32,35},{40,43},{64,67},{72,75},{96,99},{104,107},{12... | collective-permute-start | bytes 2359304 | tf_op jit(solution)/shard_map/ppermute | solution.py:28
  78.4 16.5 %collective-permute-done.10.refs_2_ = f32[2,2,192,256]{3,2,1,0:T(8,128)S(1)} collective-permute-done((f32[2,2,192,256]{3,2,1,0:T(8,128)S(1)}, f32[2,2,192,256]{3,2,1,0:T(8,128)S(1)}, u32[]{:S(2)}, u32[]{:S(2)}) %collective-permute-start.10) | collective-permute-done | bytes 786464 | tf_op jit(solution)/shard_map/ppermute | solution.py:28
  94.9 1.6 %split_shots.1 = (bf16[768,2048]{1,0:T(8,128)(2,1)S(1)}, bf16[768,2048]{1,0:T(8,128)(2,1)S(1)}) custom-call(f32[2,2,192,256]{3,2,1,0:T(8,128)S(1)} %pad_maximum_fusion.refs_0_, f32[2,2,192,256]{3,2,1,0:T(8,128)S(1)} %collective-permute-done.6.refs_1_, f32[2,2,192,256]{3,2,1,0:T(8,128)S(1)} %collective-permute-done.10.refs_2_, ...), custom_call_target="tpu_custom_call" | custom-call | bytes 12582912 | tf_op jit(solution)/shard_map/split_shots/pallas_call | solution.py:133
  96.5 1.7 %copy-done.1 = bf16[768,2048]{1,0:T(8,128)(2,1)} copy-done((bf16[768,2048]{1,0:T(8,128)(2,1)}, bf16[768,2048]{1,0:T(8,128)(2,1)S(1)}, u32[]{:S(2)}) %copy-start.1) | copy-done | bytes 3145752
  98.2 3.4 %copy-done = f32[64,256,128]{2,1,0:T(8,128)S(1)} copy-done((f32[64,256,128]{2,1,0:T(8,128)S(1)}, f32[64,256,128]{2,1,0:T(8,128)}, u32[]{:S(2)}) %copy-start) | copy-done | bytes 8388632
  101.6 1.9 %copy-done.2 = bf16[768,2048]{1,0:T(8,128)(2,1)S(1)} copy-done((bf16[768,2048]{1,0:T(8,128)(2,1)S(1)}, bf16[768,2048]{1,0:T(8,128)(2,1)}, u32[]{:S(2)}) %copy-start.2) | copy-done | bytes 3145752
  103.5 11.0 %products.1 = f32[16,192,128]{2,1,0:T(8,128)S(1)} custom-call(f32[64,256,128]{2,1,0:T(8,128)S(1)} %copy-done, bf16[768,2048]{1,0:T(8,128)(2,1)S(1)} %get-tuple-element.31.high_ref, bf16[768,2048]{1,0:T(8,128)(2,1)S(1)} %copy-done.2), custom_call_target="tpu_custom_call" | custom-call | flops 9663676416 | bytes 15728640 | tf_op jit(solution)/shard_map/products/pallas_call | solution.py:182
  114.4 26.9 %all_to_all.5.came = f32[16,192,128]{2,1,0:T(8,128)S(1)} all-to-all(f32[16,192,128]{2,1,0:T(8,128)S(1)} %products.1), channel_id=1, replica_groups={{0,1,2,3,4,5,6,7,16,17,18,19,20,21,22,23},{8,9,10,11,12,13,14,15,24,25,..., dimensions={0} | all-to-all | bytes 3145728 | tf_op jit(solution)/shard_map/all_to_all | solution.py:60
  141.3 1.6 %finish.1 = f32[2,2,192,512]{3,2,1,0:T(8,128)} custom-call(f32[16,192,128]{2,1,0:T(8,128)S(1)} %all_to_all.5.came), custom_call_target="tpu_custom_call" | custom-call | bytes 3145728 | tf_op jit(solution)/shard_map/finish/pallas_call | solution.py:207
  (17 shorter events, 0.4 us)
Async XLA Ops:
  6.5 91.7 %all-gather.2.cloned.1.call-start = ((), (), s32[]{:S(2)}) async-start(), calls=%async_computation.1 | async-start | bytes 8912896 | tf_op jit(solution)/shard_map/all_gather | solution.py:51
  7.7 26.6 %collective-permute-start.4 = (f32[2,192,256]{2,1,0:T(8,128)S(1)}, f32[2,192,256]{2,1,0:T(8,128)S(1)}, u32[]{:S(2)}, u32[]{:S(2)}) collective-permute-start(f32[2,192,256]{2,1,0:T(8,128)S(1)} %get-tuple-element.34), channel_id=1, source_target_pairs={{0,16},{8,24},{32,48},{40,56},{64,80},{72,88},{96,112},{104,120},{... | collective-permute-start | bytes 1179656 | tf_op jit(solution)/shard_map/ppermute | solution.py:28
  13.5 9.6 %collective-permute-start = (f32[256,128]{1,0:T(8,128)}, f32[256,128]{1,0:T(8,128)S(1)}, u32[]{:S(2)}, u32[]{:S(2)}) collective-permute-start(f32[256,128]{1,0:T(8,128)} %get-tuple-element.19), channel_id=1, source_target_pairs={{0,0},{8,2},{32,32},{40,34},{64,64},{72,66},{96,96},{104,98},{128,... | collective-permute-start | bytes 393224 | tf_op jit(solution)/shard_map/ppermute | solution.py:28
  19.0 7.2 %collective-permute-start.1 = (f32[256,128]{1,0:T(8,128)}, f32[256,128]{1,0:T(8,128)S(1)}, u32[]{:S(2)}, u32[]{:S(2)}) collective-permute-start(f32[256,128]{1,0:T(8,128)} %get-tuple-element.20), channel_id=1, source_target_pairs={{0,4},{8,6},{32,36},{40,38},{64,68},{72,70},{96,100},{104,102},{12... | collective-permute-start | bytes 393224 | tf_op jit(solution)/shard_map/ppermute | solution.py:28
  19.2 11.9 %collective-permute-start.2 = (f32[256,128]{1,0:T(8,128)}, f32[256,128]{1,0:T(8,128)S(1)}, u32[]{:S(2)}, u32[]{:S(2)}) collective-permute-start(f32[256,128]{1,0:T(8,128)} %get-tuple-element.21), channel_id=1, source_target_pairs={{0,16},{8,18},{32,48},{40,50},{64,80},{72,82},{96,112},{104,114},{... | collective-permute-start | bytes 393224 | tf_op jit(solution)/shard_map/ppermute | solution.py:28
  23.1 10.4 %collective-permute-start.3 = (f32[256,128]{1,0:T(8,128)}, f32[256,128]{1,0:T(8,128)S(1)}, u32[]{:S(2)}, u32[]{:S(2)}) collective-permute-start(f32[256,128]{1,0:T(8,128)} %get-tuple-element.22), channel_id=1, source_target_pairs={{0,20},{8,22},{32,52},{40,54},{64,84},{72,86},{96,116},{104,118},{... | collective-permute-start | bytes 393224 | tf_op jit(solution)/shard_map/ppermute | solution.py:28
  34.4 19.5 %collective-permute-start.5 = (f32[2,2,192,256]{3,2,1,0:T(8,128)S(1)}, f32[2,2,192,256]{3,2,1,0:T(8,128)S(1)}, u32[]{:S(2)}, u32[]{:S(2)}) collective-permute-start(f32[2,2,192,256]{3,2,1,0:T(8,128)S(1)} %pad_maximum_fusion.refs_0_), channel_id=1, source_target_pairs={{0,4},{8,12},{32,36},{40,44},{64,68},{72,76},{96,100},{104,108},{1... | collective-permute-start | bytes 2359304 | tf_op jit(solution)/shard_map/ppermute | solution.py:28
  34.7 20.8 %collective-permute-start.6 = (f32[2,2,192,256]{3,2,1,0:T(8,128)S(1)}, f32[2,2,192,256]{3,2,1,0:T(8,128)S(1)}, u32[]{:S(2)}, u32[]{:S(2)}) collective-permute-start(f32[2,2,192,256]{3,2,1,0:T(8,128)S(1)} %pad_maximum_fusion.refs_0_), channel_id=1, source_target_pairs={{0,1},{8,9},{32,33},{40,41},{64,65},{72,73},{96,97},{104,105},{128... | collective-permute-start | bytes 2359304 | tf_op jit(solution)/shard_map/ppermute | solution.py:28
  34.7 20.8 %collective-permute-start.7 = (f32[2,2,192,256]{3,2,1,0:T(8,128)S(1)}, f32[2,2,192,256]{3,2,1,0:T(8,128)S(1)}, u32[]{:S(2)}, u32[]{:S(2)}) collective-permute-start(f32[2,2,192,256]{3,2,1,0:T(8,128)S(1)} %pad_maximum_fusion.refs_0_), channel_id=1, source_target_pairs={{0,3},{8,11},{32,35},{40,43},{64,67},{72,75},{96,99},{104,107},{12... | collective-permute-start | bytes 2359304 | tf_op jit(solution)/shard_map/ppermute | solution.py:28
  55.6 20.1 %collective-permute-start.8 = (f32[2,2,192,256]{3,2,1,0:T(8,128)S(1)}, f32[2,2,192,256]{3,2,1,0:T(8,128)S(1)}, u32[]{:S(2)}, u32[]{:S(2)}) collective-permute-start(f32[2,2,192,256]{3,2,1,0:T(8,128)S(1)} %collective-permute-done.5.refs_4_), channel_id=1, source_target_pairs={{0,1},{8,9},{32,33},{40,41},{64,65},{72,73},{96,97},{104,105},{128... | collective-permute-start | bytes 2359304 | tf_op jit(solution)/shard_map/ppermute | solution.py:28
  55.6 20.1 %collective-permute-start.9 = (f32[2,2,192,256]{3,2,1,0:T(8,128)S(1)}, f32[2,2,192,256]{3,2,1,0:T(8,128)S(1)}, u32[]{:S(2)}, u32[]{:S(2)}) collective-permute-start(f32[2,2,192,256]{3,2,1,0:T(8,128)S(1)} %collective-permute-done.5.refs_4_), channel_id=1, source_target_pairs={{0,3},{8,11},{32,35},{40,43},{64,67},{72,75},{96,99},{104,107},{12... | collective-permute-start | bytes 2359304 | tf_op jit(solution)/shard_map/ppermute | solution.py:28
  75.7 19.2 %collective-permute-start.10 = (f32[2,2,192,256]{3,2,1,0:T(8,128)S(1)}, f32[2,2,192,256]{3,2,1,0:T(8,128)S(1)}, u32[]{:S(2)}, u32[]{:S(2)}) collective-permute-start(f32[2,2,192,256]{3,2,1,0:T(8,128)S(1)} %collective-permute-done.6.refs_1_), channel_id=1, source_target_pairs={{0,1},{8,9},{32,33},{40,41},{64,65},{72,73},{96,97},{104,105},{128... | collective-permute-start | bytes 2359304 | tf_op jit(solution)/shard_map/ppermute | solution.py:28
  75.8 19.1 %collective-permute-start.11 = (f32[2,2,192,256]{3,2,1,0:T(8,128)S(1)}, f32[2,2,192,256]{3,2,1,0:T(8,128)S(1)}, u32[]{:S(2)}, u32[]{:S(2)}) collective-permute-start(f32[2,2,192,256]{3,2,1,0:T(8,128)S(1)} %collective-permute-done.9.refs_7_), channel_id=1, source_target_pairs={{0,3},{8,11},{32,35},{40,43},{64,67},{72,75},{96,99},{104,107},{12... | collective-permute-start | bytes 2359304 | tf_op jit(solution)/shard_map/ppermute | solution.py:28
  96.5 1.7 %copy-start.1 = (bf16[768,2048]{1,0:T(8,128)(2,1)}, bf16[768,2048]{1,0:T(8,128)(2,1)S(1)}, u32[]{:S(2)}) copy-start(bf16[768,2048]{1,0:T(8,128)(2,1)S(1)} %get-tuple-element.32.low_ref) | copy-start | bytes 9437188
  98.2 3.4 %copy-start = (f32[64,256,128]{2,1,0:T(8,128)S(1)}, f32[64,256,128]{2,1,0:T(8,128)}, u32[]{:S(2)}) copy-start(f32[64,256,128]{2,1,0:T(8,128)} %all-gather.2.cloned.1.call-done.gathered) | copy-start | bytes 25165828
  101.6 1.9 %copy-start.2 = (bf16[768,2048]{1,0:T(8,128)(2,1)S(1)}, bf16[768,2048]{1,0:T(8,128)(2,1)}, u32[]{:S(2)}) copy-start(bf16[768,2048]{1,0:T(8,128)(2,1)} %copy-done.1) | copy-start | bytes 9437188
Sparse Core Ops, SparseCore 0:
  34.4 58.0 all-gather.1
